TPU v7x, 32 devices: a whole 2x2x4 slice. The times are simulated.
32 devices in a mesh: section: 4 (over z), dom: 8 (over y, x, core).
Axes of the slice: x: 2, y: 2, z: 4, core: 2. Of those that a mesh axis runs over, the one named last changes fastest.
Arguments:
- images: bfloat16 [4, 32, 65536], P('section', None, 'dom'), may hold values from -48 to 48
- weights: bfloat16 [8, 1024, 64, 256], P('section', 'dom'), may hold values from -0.625 to 0.625
- bias: bfloat16 [8, 65536], P('section', 'dom'), may hold values from -12 to 12
- pattern: int32 [8, 1024, 4], P('section'), may hold values from 0 to 1023, as said below
- counts: int32 [8, 1024], P('section', 'dom'), may hold values from 2 to 4, as said below
Outputs:
- scores: bfloat16 [4, 32, 65536], P('section', None, 'dom')
Inputs may be any that keep to these rules, and one draw needn't show every extreme that they name: `pattern`: A partition is the 128 consecutive column blocks of one neuron partition (and the row blocks of the same numbers). In each layer, slot 0 of every column block names a row block of its own partition; all slots of one partition's column blocks that name a row block of another partition name the same block of that partition, and every other partition is named so by slot 1 of some column block. Only the first counts[l, n] slots of a column block are live. In each layer every partition has a column block with all 4 slots live.
All inputs are finite; a program needn't handle non-finite values.
Results may differ from a plain program's by a relative error of at most 0.02.
Values may be sent and summed in bfloat16 or wider, within the bound.
A program may use at most 128 MiB of HBM per device.

v0:
```python
import jax
import jax.numpy as jnp
from jax import lax
from jax.sharding import PartitionSpec as P


def passed_along(x, axis, by):
    length = lax.axis_size(axis)
    pairs = [(i, i + by) for i in range(length) if 0 <= i + by < length]
    return lax.ppermute(x, axis, pairs)


def spread(x, axis, root):
    mine = lax.axis_index(axis) == root
    return lax.psum(jnp.where(mine, x, jnp.zeros_like(x)), axis)


def prepare_tables(weights, pattern, counts, part_count, my_part):
    layer_count = weights.shape[0]
    per_part = weights.shape[1]
    block_size = weights.shape[2]
    slot_count = pattern.shape[2]
    block_table = pattern.reshape(layer_count, part_count, per_part * slot_count)
    owners = block_table // per_part
    wanted = jnp.max(jnp.where(owners == my_part, block_table % per_part, 0), axis=2)
    own_rows = lax.dynamic_slice_in_dim(pattern, my_part * per_part, per_part, 1)
    own_owners = own_rows // per_part
    source = jnp.where(own_owners == my_part, own_rows % per_part, per_part + own_owners)
    live_slots = (jnp.arange(slot_count)[None, None, :] < counts[:, :, None]).astype(weights.dtype)
    masked = (
        weights.reshape(layer_count, per_part, block_size, slot_count, block_size)
        * live_slots[:, :, None, :, None]
    )
    return (wanted, source, masked.reshape(weights.shape))


def apply_layer(current, wanted_row, layer_source, weight_layer, bias_row, part_count):
    image_rows = current.shape[0]
    local_width = current.shape[1]
    per_part = weight_layer.shape[0]
    block_size = weight_layer.shape[1]
    slot_count = layer_source.shape[1]
    blocks = current.reshape(image_rows, per_part, block_size)
    outgoing = jnp.take(blocks, wanted_row, axis=1).reshape(image_rows, part_count * block_size)
    arrived = lax.all_to_all(outgoing, "dom", split_axis=1, concat_axis=1, tiled=True)
    pooled = jnp.concatenate([blocks, arrived.reshape(image_rows, part_count, block_size)], axis=1)
    picked = jnp.take(pooled, layer_source.reshape(-1), axis=1)
    picked = picked.reshape(image_rows, per_part, slot_count * block_size)
    summed = jnp.einsum("bck,cok->bco", picked, weight_layer, preferred_element_type=jnp.float32)
    pre_act = summed.reshape(image_rows, local_width) + bias_row.astype(jnp.float32)[None, :]
    return jnp.clip(pre_act, 0.0, 32.0).astype(jnp.bfloat16)


def shards(images, weights, bias, pattern, counts):
    section_count = lax.axis_size("section")
    part_count = lax.axis_size("dom")
    my_part = lax.axis_index("dom")
    my_section = lax.axis_index("section")
    image_rows = images.shape[1]
    local_width = images.shape[2]
    wanted, source, masked = prepare_tables(weights, pattern, counts, part_count, my_part)
    layer_count = weights.shape[0]
    fed_images = lax.all_gather(images, "section", axis=0, tiled=True)
    micro_count = fed_images.shape[0]

    def pipe_step(time_idx, state_pair):
        incoming, results = state_pair
        entering = lax.dynamic_index_in_dim(
            fed_images, jnp.minimum(time_idx, micro_count - 1), 0, keepdims=False
        )
        current = jnp.where(my_section == 0, entering, incoming)
        for layer_idx in range(layer_count):
            current = apply_layer(
                current,
                wanted[layer_idx],
                source[layer_idx],
                masked[layer_idx],
                bias[layer_idx],
                part_count,
            )
        micro_idx = time_idx - (section_count - 1)
        keep_flag = (my_section == section_count - 1) & (micro_idx >= 0)
        slot_index = jnp.clip(micro_idx, 0, micro_count - 1)
        previous = lax.dynamic_index_in_dim(results, slot_index, 0, keepdims=False)
        results = lax.dynamic_update_index_in_dim(
            results, jnp.where(keep_flag, current, previous), slot_index, 0
        )
        passed = passed_along(current, "section", 1)
        return (passed, results)

    initial = (
        jnp.zeros((image_rows, local_width), jnp.bfloat16),
        jnp.zeros((micro_count, image_rows, local_width), jnp.bfloat16),
    )
    _, results = lax.fori_loop(0, micro_count + section_count - 1, pipe_step, initial)
    delivered = spread(results, "section", section_count - 1)
    return lax.dynamic_slice_in_dim(delivered, my_section * images.shape[0], images.shape[0], 0)


def solution(mesh):
    placed = (
        P("section", None, "dom"),
        P("section", "dom", None, None),
        P("section", "dom"),
        P("section", None, None),
        P("section", "dom"),
    )
    return jax.shard_map(
        shards, mesh=mesh, in_specs=placed, out_specs=P("section", None, "dom"), check_vma=False
    )
```

profile of v0, /device:TPU:25, one launch (start us, length us, event | category | flops | bytes accessed | tf_op | source)
XLA Modules:
  0.0 718.8 jit_solution(9825836031195446295)
XLA Ops:
  10.1 7.2 %broadcast_multiply_fusion = bf16[2,128,64,256]{3,2,1,0:T(8,128)(2,1)} fusion(bf16[2,128,64,256]{3,2,1,0:T(8,128)(2,1)} %param.12, bf16[2,128,256]{2,1,0:T(8,128)(2,1)S(1)} %copy.35), kind=kLoop, calls=%fused_computation.40 | loop fusion | flops 4194304 | bytes 16908288 | tf_op jit(solution)/shard_map/mul | solution.py:31
  17.3 36.6 %all-gather.2.cloned.1.call-done = bf16[4,32,8192]{2,1,0:T(8,128)(2,1)} async-done(((bf16[1,32,8192]{2,1,0:T(8,128)(2,1)}), bf16[4,32,8192]{2,1,0:T(8,128)(2,1)}) %all-gather.2.cloned.1.call-update) | async-done | bytes 2097168 | tf_op jit(solution)/shard_map/all_gather | solution.py:63
  55.5 566.2 %while.17 = (s32[]{:T(128)}, bf16[32,8192]{1,0:T(8,128)(2,1)S(1)}, bf16[4,32,8192]{2,1,0:T(8,128)(2,1)}, pred[]{:T(512)}, bf16[4,32,8192]{2,1,0:T(8,128)(2,1)}, ...) while((s32[]{:T(128)}, bf16[32,8192]{1,0:T(8,128)(2,1)S(1)}, ...), condition=%wide.region_3.6_spmd, body=%wide.region_2.5_spmd.sunk | while | flops 274035808 | bytes 70900376 | solution.py:95
  59.8 4.1 all-to-all-start
  78.6 5.5 reshape.235
  108.1 5.5 reshape.239
  124.4 11.2 %collective-permute-done = bf16[32,8192]{1,0:T(8,128)(2,1)S(1)} collective-permute-done((bf16[32,8192]{1,0:T(8,128)(2,1)S(1)}, bf16[32,8192]{1,0:T(8,128)(2,1)S(1)}, u32[]{:S(2)}, u32[]{:S(2)}) %collective-permute-start) | collective-permute-done | bytes 524320 | tf_op jit(solution)/shard_map/while/body/eval_jaxpr/ppermute | solution.py:10
  140.0 4.9 all-to-all-start
  159.6 5.5 reshape.235
  189.1 5.5 reshape.239
  205.4 11.2 %collective-permute-done = bf16[32,8192]{1,0:T(8,128)(2,1)S(1)} collective-permute-done((bf16[32,8192]{1,0:T(8,128)(2,1)S(1)}, bf16[32,8192]{1,0:T(8,128)(2,1)S(1)}, u32[]{:S(2)}, u32[]{:S(2)}) %collective-permute-start) | collective-permute-done | bytes 524320 | tf_op jit(solution)/shard_map/while/body/eval_jaxpr/ppermute | solution.py:10
  221.0 4.9 all-to-all-start
  240.6 5.5 reshape.235
  270.1 5.5 reshape.239
  286.4 11.2 %collective-permute-done = bf16[32,8192]{1,0:T(8,128)(2,1)S(1)} collective-permute-done((bf16[32,8192]{1,0:T(8,128)(2,1)S(1)}, bf16[32,8192]{1,0:T(8,128)(2,1)S(1)}, u32[]{:S(2)}, u32[]{:S(2)}) %collective-permute-start) | collective-permute-done | bytes 524320 | tf_op jit(solution)/shard_map/while/body/eval_jaxpr/ppermute | solution.py:10
  302.0 4.9 all-to-all-start
  321.6 5.5 reshape.235
  351.1 5.5 reshape.239
  367.4 11.2 %collective-permute-done = bf16[32,8192]{1,0:T(8,128)(2,1)S(1)} collective-permute-done((bf16[32,8192]{1,0:T(8,128)(2,1)S(1)}, bf16[32,8192]{1,0:T(8,128)(2,1)S(1)}, u32[]{:S(2)}, u32[]{:S(2)}) %collective-permute-start) | collective-permute-done | bytes 524320 | tf_op jit(solution)/shard_map/while/body/eval_jaxpr/ppermute | solution.py:10
  383.0 4.9 all-to-all-start
  402.6 5.5 reshape.235
  432.1 5.5 reshape.239
  448.4 11.2 %collective-permute-done = bf16[32,8192]{1,0:T(8,128)(2,1)S(1)} collective-permute-done((bf16[32,8192]{1,0:T(8,128)(2,1)S(1)}, bf16[32,8192]{1,0:T(8,128)(2,1)S(1)}, u32[]{:S(2)}, u32[]{:S(2)}) %collective-permute-start) | collective-permute-done | bytes 524320 | tf_op jit(solution)/shard_map/while/body/eval_jaxpr/ppermute | solution.py:10
  464.0 4.9 all-to-all-start
  483.6 5.5 reshape.235
  513.1 5.5 reshape.239
  529.4 11.3 %collective-permute-done = bf16[32,8192]{1,0:T(8,128)(2,1)S(1)} collective-permute-done((bf16[32,8192]{1,0:T(8,128)(2,1)S(1)}, bf16[32,8192]{1,0:T(8,128)(2,1)S(1)}, u32[]{:S(2)}, u32[]{:S(2)}) %collective-permute-start) | collective-permute-done | bytes 524320 | tf_op jit(solution)/shard_map/while/body/eval_jaxpr/ppermute | solution.py:10
  545.0 4.9 all-to-all-start
  564.6 5.5 reshape.235
  594.1 5.5 reshape.239
  610.4 11.2 %collective-permute-done = bf16[32,8192]{1,0:T(8,128)(2,1)S(1)} collective-permute-done((bf16[32,8192]{1,0:T(8,128)(2,1)S(1)}, bf16[32,8192]{1,0:T(8,128)(2,1)S(1)}, u32[]{:S(2)}, u32[]{:S(2)}) %collective-permute-start) | collective-permute-done | bytes 524320 | tf_op jit(solution)/shard_map/while/body/eval_jaxpr/ppermute | solution.py:10
  624.7 85.3 %all-reduce.2.cloned.1.call-done = bf16[4,32,8192]{2,1,0:T(8,128)(2,1)} async-done(((bf16[4,32,8192]{2,1,0:T(8,128)(2,1)}), bf16[4,32,8192]{2,1,0:T(8,128)(2,1)}) %all-reduce.2.cloned.1.call-update) | async-done | bytes 2097168 | tf_op jit(solution)/shard_map/psum | solution.py:15
  (340 shorter events, 385.6 us)
Async XLA Ops:
  6.5 47.4 %all-gather.2.cloned.1.call-start = ((), (), s32[]{:S(2)}) async-start(), calls=%async_computation.2 | async-start | bytes 2621440 | tf_op jit(solution)/shard_map/all_gather | solution.py:63
  7.3 702.8 %all-reduce.2.cloned.1.call-start = ((), (), s32[]{:S(2)}) async-start(), calls=%async_computation.3 | async-start | bytes 4194304 | tf_op jit(solution)/shard_map/psum | solution.py:15
  17.3 38.2 %copy-start.1 = (bf16[2,8192]{1,0:T(2,128)(2,1)S(1)}, bf16[2,8192]{1,0:T(2,128)(2,1)}, u32[]{:S(2)}) copy-start(bf16[2,8192]{1,0:T(2,128)(2,1)} %param.13) | copy-start | bytes 98308
  59.8 8.2 %all-to-all-start = ((bf16[8,2,1024]{2,1,0:T(2,128)(2,1)}), bf16[8,2,1024]{2,1,0:T(2,128)(2,1)S(1)}, u32[]{:S(2)}, u32[]{:S(2)}) async-start(bf16[8,2,1024]{2,1,0:T(2,128)(2,1)} %reshape.233), calls=%async_computation | async-start | bytes 65536 | tf_op jit(solution)/shard_map/while/body/eval_jaxpr/all_to_all | solution.py:45
  89.3 8.1 %all-to-all-start.1 = ((bf16[8,2,1024]{2,1,0:T(2,128)(2,1)}), bf16[8,2,1024]{2,1,0:T(2,128)(2,1)S(1)}, u32[]{:S(2)}, u32[]{:S(2)}) async-start(bf16[8,2,1024]{2,1,0:T(2,128)(2,1)} %reshape.237), calls=%async_computation.1 | async-start | bytes 65536 | tf_op jit(solution)/shard_map/while/body/eval_jaxpr/all_to_all | solution.py:45
  120.9 1.5 copy-start
  121.0 14.7 %collective-permute-start = (bf16[32,8192]{1,0:T(8,128)(2,1)S(1)}, bf16[32,8192]{1,0:T(8,128)(2,1)S(1)}, u32[]{:S(2)}, u32[]{:S(2)}) collective-permute-start(bf16[32,8192]{1,0:T(8,128)(2,1)S(1)} %clamp_convert_fusion.4), channel_id=1, source_target_pairs={{0,8},{8,16},{16,24},{1,9},{9,17},{17,25},{2,10},{10,18},{18,26},{... | collective-permute-start | bytes 1572872 | tf_op jit(solution)/shard_map/while/body/eval_jaxpr/ppermute | solution.py:10
  140.0 9.0 %all-to-all-start = ((bf16[8,2,1024]{2,1,0:T(2,128)(2,1)}), bf16[8,2,1024]{2,1,0:T(2,128)(2,1)S(1)}, u32[]{:S(2)}, u32[]{:S(2)}) async-start(bf16[8,2,1024]{2,1,0:T(2,128)(2,1)} %reshape.233), calls=%async_computation | async-start | bytes 65536 | tf_op jit(solution)/shard_map/while/body/eval_jaxpr/all_to_all | solution.py:45
  170.3 8.1 %all-to-all-start.1 = ((bf16[8,2,1024]{2,1,0:T(2,128)(2,1)}), bf16[8,2,1024]{2,1,0:T(2,128)(2,1)S(1)}, u32[]{:S(2)}, u32[]{:S(2)}) async-start(bf16[8,2,1024]{2,1,0:T(2,128)(2,1)} %reshape.237), calls=%async_computation.1 | async-start | bytes 65536 | tf_op jit(solution)/shard_map/while/body/eval_jaxpr/all_to_all | solution.py:45
  201.9 1.5 copy-start
  202.0 14.7 %collective-permute-start = (bf16[32,8192]{1,0:T(8,128)(2,1)S(1)}, bf16[32,8192]{1,0:T(8,128)(2,1)S(1)}, u32[]{:S(2)}, u32[]{:S(2)}) collective-permute-start(bf16[32,8192]{1,0:T(8,128)(2,1)S(1)} %clamp_convert_fusion.4), channel_id=1, source_target_pairs={{0,8},{8,16},{16,24},{1,9},{9,17},{17,25},{2,10},{10,18},{18,26},{... | collective-permute-start | bytes 1572872 | tf_op jit(solution)/shard_map/while/body/eval_jaxpr/ppermute | solution.py:10
  221.0 9.0 %all-to-all-start = ((bf16[8,2,1024]{2,1,0:T(2,128)(2,1)}), bf16[8,2,1024]{2,1,0:T(2,128)(2,1)S(1)}, u32[]{:S(2)}, u32[]{:S(2)}) async-start(bf16[8,2,1024]{2,1,0:T(2,128)(2,1)} %reshape.233), calls=%async_computation | async-start | bytes 65536 | tf_op jit(solution)/shard_map/while/body/eval_jaxpr/all_to_all | solution.py:45
  251.3 8.1 %all-to-all-start.1 = ((bf16[8,2,1024]{2,1,0:T(2,128)(2,1)}), bf16[8,2,1024]{2,1,0:T(2,128)(2,1)S(1)}, u32[]{:S(2)}, u32[]{:S(2)}) async-start(bf16[8,2,1024]{2,1,0:T(2,128)(2,1)} %reshape.237), calls=%async_computation.1 | async-start | bytes 65536 | tf_op jit(solution)/shard_map/while/body/eval_jaxpr/all_to_all | solution.py:45
  282.9 1.5 copy-start
  283.0 14.7 %collective-permute-start = (bf16[32,8192]{1,0:T(8,128)(2,1)S(1)}, bf16[32,8192]{1,0:T(8,128)(2,1)S(1)}, u32[]{:S(2)}, u32[]{:S(2)}) collective-permute-start(bf16[32,8192]{1,0:T(8,128)(2,1)S(1)} %clamp_convert_fusion.4), channel_id=1, source_target_pairs={{0,8},{8,16},{16,24},{1,9},{9,17},{17,25},{2,10},{10,18},{18,26},{... | collective-permute-start | bytes 1572872 | tf_op jit(solution)/shard_map/while/body/eval_jaxpr/ppermute | solution.py:10
  302.0 9.0 %all-to-all-start = ((bf16[8,2,1024]{2,1,0:T(2,128)(2,1)}), bf16[8,2,1024]{2,1,0:T(2,128)(2,1)S(1)}, u32[]{:S(2)}, u32[]{:S(2)}) async-start(bf16[8,2,1024]{2,1,0:T(2,128)(2,1)} %reshape.233), calls=%async_computation | async-start | bytes 65536 | tf_op jit(solution)/shard_map/while/body/eval_jaxpr/all_to_all | solution.py:45
  332.3 8.1 %all-to-all-start.1 = ((bf16[8,2,1024]{2,1,0:T(2,128)(2,1)}), bf16[8,2,1024]{2,1,0:T(2,128)(2,1)S(1)}, u32[]{:S(2)}, u32[]{:S(2)}) async-start(bf16[8,2,1024]{2,1,0:T(2,128)(2,1)} %reshape.237), calls=%async_computation.1 | async-start | bytes 65536 | tf_op jit(solution)/shard_map/while/body/eval_jaxpr/all_to_all | solution.py:45
  363.9 1.5 copy-start
  364.0 14.7 %collective-permute-start = (bf16[32,8192]{1,0:T(8,128)(2,1)S(1)}, bf16[32,8192]{1,0:T(8,128)(2,1)S(1)}, u32[]{:S(2)}, u32[]{:S(2)}) collective-permute-start(bf16[32,8192]{1,0:T(8,128)(2,1)S(1)} %clamp_convert_fusion.4), channel_id=1, source_target_pairs={{0,8},{8,16},{16,24},{1,9},{9,17},{17,25},{2,10},{10,18},{18,26},{... | collective-permute-start | bytes 1572872 | tf_op jit(solution)/shard_map/while/body/eval_jaxpr/ppermute | solution.py:10
  383.0 9.0 %all-to-all-start = ((bf16[8,2,1024]{2,1,0:T(2,128)(2,1)}), bf16[8,2,1024]{2,1,0:T(2,128)(2,1)S(1)}, u32[]{:S(2)}, u32[]{:S(2)}) async-start(bf16[8,2,1024]{2,1,0:T(2,128)(2,1)} %reshape.233), calls=%async_computation | async-start | bytes 65536 | tf_op jit(solution)/shard_map/while/body/eval_jaxpr/all_to_all | solution.py:45
  413.3 8.1 %all-to-all-start.1 = ((bf16[8,2,1024]{2,1,0:T(2,128)(2,1)}), bf16[8,2,1024]{2,1,0:T(2,128)(2,1)S(1)}, u32[]{:S(2)}, u32[]{:S(2)}) async-start(bf16[8,2,1024]{2,1,0:T(2,128)(2,1)} %reshape.237), calls=%async_computation.1 | async-start | bytes 65536 | tf_op jit(solution)/shard_map/while/body/eval_jaxpr/all_to_all | solution.py:45
  444.9 1.5 copy-start
  445.0 14.7 %collective-permute-start = (bf16[32,8192]{1,0:T(8,128)(2,1)S(1)}, bf16[32,8192]{1,0:T(8,128)(2,1)S(1)}, u32[]{:S(2)}, u32[]{:S(2)}) collective-permute-start(bf16[32,8192]{1,0:T(8,128)(2,1)S(1)} %clamp_convert_fusion.4), channel_id=1, source_target_pairs={{0,8},{8,16},{16,24},{1,9},{9,17},{17,25},{2,10},{10,18},{18,26},{... | collective-permute-start | bytes 1572872 | tf_op jit(solution)/shard_map/while/body/eval_jaxpr/ppermute | solution.py:10
  464.0 9.0 %all-to-all-start = ((bf16[8,2,1024]{2,1,0:T(2,128)(2,1)}), bf16[8,2,1024]{2,1,0:T(2,128)(2,1)S(1)}, u32[]{:S(2)}, u32[]{:S(2)}) async-start(bf16[8,2,1024]{2,1,0:T(2,128)(2,1)} %reshape.233), calls=%async_computation | async-start | bytes 65536 | tf_op jit(solution)/shard_map/while/body/eval_jaxpr/all_to_all | solution.py:45
  494.3 8.1 %all-to-all-start.1 = ((bf16[8,2,1024]{2,1,0:T(2,128)(2,1)}), bf16[8,2,1024]{2,1,0:T(2,128)(2,1)S(1)}, u32[]{:S(2)}, u32[]{:S(2)}) async-start(bf16[8,2,1024]{2,1,0:T(2,128)(2,1)} %reshape.237), calls=%async_computation.1 | async-start | bytes 65536 | tf_op jit(solution)/shard_map/while/body/eval_jaxpr/all_to_all | solution.py:45
  525.9 1.5 copy-start
  526.0 14.7 %collective-permute-start = (bf16[32,8192]{1,0:T(8,128)(2,1)S(1)}, bf16[32,8192]{1,0:T(8,128)(2,1)S(1)}, u32[]{:S(2)}, u32[]{:S(2)}) collective-permute-start(bf16[32,8192]{1,0:T(8,128)(2,1)S(1)} %clamp_convert_fusion.4), channel_id=1, source_target_pairs={{0,8},{8,16},{16,24},{1,9},{9,17},{17,25},{2,10},{10,18},{18,26},{... | collective-permute-start | bytes 1572872 | tf_op jit(solution)/shard_map/while/body/eval_jaxpr/ppermute | solution.py:10
  545.0 9.0 %all-to-all-start = ((bf16[8,2,1024]{2,1,0:T(2,128)(2,1)}), bf16[8,2,1024]{2,1,0:T(2,128)(2,1)S(1)}, u32[]{:S(2)}, u32[]{:S(2)}) async-start(bf16[8,2,1024]{2,1,0:T(2,128)(2,1)} %reshape.233), calls=%async_computation | async-start | bytes 65536 | tf_op jit(solution)/shard_map/while/body/eval_jaxpr/all_to_all | solution.py:45
  575.3 8.1 %all-to-all-start.1 = ((bf16[8,2,1024]{2,1,0:T(2,128)(2,1)}), bf16[8,2,1024]{2,1,0:T(2,128)(2,1)S(1)}, u32[]{:S(2)}, u32[]{:S(2)}) async-start(bf16[8,2,1024]{2,1,0:T(2,128)(2,1)} %reshape.237), calls=%async_computation.1 | async-start | bytes 65536 | tf_op jit(solution)/shard_map/while/body/eval_jaxpr/all_to_all | solution.py:45
  606.8 1.5 copy-start
  607.0 14.7 %collective-permute-start = (bf16[32,8192]{1,0:T(8,128)(2,1)S(1)}, bf16[32,8192]{1,0:T(8,128)(2,1)S(1)}, u32[]{:S(2)}, u32[]{:S(2)}) collective-permute-start(bf16[32,8192]{1,0:T(8,128)(2,1)S(1)} %clamp_convert_fusion.4), channel_id=1, source_target_pairs={{0,8},{8,16},{16,24},{1,9},{9,17},{17,25},{2,10},{10,18},{18,26},{... | collective-permute-start | bytes 1572872 | tf_op jit(solution)/shard_map/while/body/eval_jaxpr/ppermute | solution.py:10
Sparse Core Ops, SparseCore 0:
  8.9 44.9 all-gather.1
  624.9 85.1 all-reduce.1
where the time goes:
time: 726 us; the launch traced here: 719 us
  waiting for transfers between devices  255 us (35%)
  local copies, waits for them, and re-layouts  239 us (33%)
  other arithmetic  85.3 us (12%)
  starting transfers between devices  71.7 us (10%)
  matrix products  52.6 us (7%)
  between operations  13.5 us (2%)
    psum x1, waiting for transfers between devices, spread(): return lax.psum(jnp.where(mine, x, jnp.zeros_like(x)), axis)  85.3 us
    ppermute x7, waiting for transfers between devices, passed_along(): return lax.ppermute(x, axis, pairs)  78.7 us
    reshape x14, local copies, waits for them, and re-layouts, apply_layer(): picked = picked.reshape(image_rows, per_part, slot_count * block_size)  76.8 us
    all_to_all x14, starting transfers between devices, apply_layer(): lax.all_to_all(outgoing, 'dom', split_axis=1, concat_axis=1, tiled=True)  61.7 us
    all_to_all x14, waiting for transfers between devices, apply_layer(): lax.all_to_all(outgoing, 'dom', split_axis=1, concat_axis=1, tiled=True)  53.7 us
    dot_general x14, matrix products, apply_layer(): jnp.einsum('bck,cok->bco', picked, weight_layer, preferred_element_type=j...  52.6 us
    select_n x14, local copies, waits for them, and re-layouts, apply_layer(): picked = jnp.take(pooled, layer_source.reshape(-1), axis=1)  50.1 us
    gather x14, local copies, waits for them, and re-layouts, apply_layer(): picked = jnp.take(pooled, layer_source.reshape(-1), axis=1)  48.5 us
  transfers between devices with their start and end apart: 23, of which 23 were waited for; matrix products, arithmetic and copies ran while one was open for 4% of the time, Pallas kernels for 0%

commit v1 on v0

v1 whole, which is shorter than its diff:
```python
import functools

import jax
import jax.numpy as jnp
from jax import lax
from jax.experimental import pallas as pl
from jax.experimental.pallas import tpu as pltpu
from jax.sharding import PartitionSpec as P

MESH = pl.DeviceIdType.MESH
CHUNKS = 4


def prepare_tables(pattern, counts, per_part, part_count, my_part):
    layer_count = pattern.shape[0]
    slot_count = pattern.shape[2]
    block_table = pattern.reshape(layer_count, part_count, per_part * slot_count)
    owners = block_table // per_part
    wanted = jnp.max(jnp.where(owners == my_part, block_table % per_part, 0), axis=2)
    own_rows = lax.dynamic_slice_in_dim(pattern, my_part * per_part, per_part, 1)
    own_owners = own_rows // per_part
    slots = jnp.arange(slot_count, dtype=jnp.int32)[None, None, :]
    local = (own_rows % per_part) ^ (slots & 1)
    remote = per_part + (my_part - own_owners + part_count) % part_count - 1
    source = jnp.where(own_owners == my_part, local, remote)
    source = jnp.where(slots < counts[:, :, None], source, per_part + part_count - 1)
    return wanted, source.reshape(layer_count, per_part * slot_count)


def kernel(
    section_count, part_count, wanted_ref, source_ref, images_ref, weights_ref, bias_ref, out_ref,
    held, inbox, outbox, table, going, coming,
    weight_sem, own_sem, feed_sem, in_sem, out_sem, result_sem, going_sem, coming_sem,
):
    my_section = lax.axis_index("section")
    me = lax.axis_index("dom")
    layer_count, quads = weights_ref.shape[0], weights_ref.shape[1]
    micro_count, tiles, rows, lanes = inbox.shape
    per_chunk = tiles // CHUNKS
    last = section_count - 1
    others = part_count - 1

    loads = [
        pltpu.make_async_copy(weights_ref.at[l], held.at[l], weight_sem.at[l])
        for l in range(layer_count)
    ]
    for load in loads:
        load.start()

    barrier = pltpu.get_barrier_semaphore()

    def greet_part(step, carry):
        pl.semaphore_signal(
            barrier, inc=1, device_id=(my_section, lax.rem(me + step, part_count)), device_id_type=MESH
        )
        return carry

    def greet_section(step, carry):
        pl.semaphore_signal(
            barrier, inc=1, device_id=(lax.rem(my_section + step, section_count), me), device_id_type=MESH
        )
        return carry

    lax.fori_loop(1, part_count, greet_part, 0)
    lax.fori_loop(1, section_count, greet_section, 0)
    pl.semaphore_wait(barrier, others + section_count - 1)

    def chunk_of(c):
        return pl.ds(c * per_chunk, per_chunk)

    def feed(c):
        return pltpu.make_async_remote_copy(
            src_ref=images_ref.at[chunk_of(c)], dst_ref=inbox.at[my_section, chunk_of(c)],
            send_sem=feed_sem.at[c], recv_sem=in_sem.at[my_section, c],
            device_id=(0, me), device_id_type=MESH,
        )

    def forward(m, c):
        return pltpu.make_async_remote_copy(
            src_ref=outbox.at[m, chunk_of(c)], dst_ref=inbox.at[m, chunk_of(c)],
            send_sem=out_sem.at[m, c], recv_sem=in_sem.at[m, c],
            device_id=(lax.rem(my_section + 1, section_count), me), device_id_type=MESH,
        )

    def deliver(m, c):
        return pltpu.make_async_remote_copy(
            src_ref=outbox.at[m, chunk_of(c)], dst_ref=out_ref.at[chunk_of(c)],
            send_sem=out_sem.at[m, c], recv_sem=result_sem.at[c],
            device_id=(m, me), device_id_type=MESH,
        )

    @pl.when(my_section != 0)
    def _():
        for c in range(CHUNKS):
            feed(c).start()

    low = lax.broadcasted_iota(jnp.int32, (rows, lanes), 1) < lanes // 2
    table[0, 2 * tiles + others] = jnp.zeros((rows, lanes), jnp.bfloat16)
    table[1, 2 * tiles + others] = jnp.zeros((rows, lanes), jnp.bfloat16)

    def turned(x):
        return pltpu.roll(x.astype(jnp.float32), lanes // 2, 1).astype(jnp.bfloat16)

    def stage(m, carry):
        @pl.when((my_section != 0) | (m != 0))
        def _():
            for c in range(CHUNKS):
                forward(m, c).wait_recv()

        @pl.when((my_section == 0) & (m == 0))
        def _():
            own = pltpu.make_async_copy(images_ref, inbox.at[0], own_sem)
            own.start()
            own.wait()
            for load in loads:
                load.wait()

        @pl.when((my_section != 0) & (m == 0))
        def _():
            for load in loads:
                load.wait()

        def enter(q, carry):
            x = inbox[m, q]
            table[0, 2 * q] = x
            table[0, 2 * q + 1] = turned(x)
            return carry

        lax.fori_loop(0, tiles, enter, 0, unroll=4)

        for l in range(layer_count):
            now, later = l % 2, (l + 1) % 2

            def send(step, carry, l=l, now=now):
                peer = lax.rem(me + step, part_count)
                block = wanted_ref[l, peer]
                going[m, l, step - 1] = jnp.where(low, table[now, block], table[now, block ^ 1])
                pltpu.make_async_remote_copy(
                    src_ref=going.at[m, l, step - 1], dst_ref=coming.at[m, l, step - 1],
                    send_sem=going_sem.at[m, l], recv_sem=coming_sem.at[m, l],
                    device_id=(my_section, peer), device_id_type=MESH,
                ).start()
                return carry

            lax.fori_loop(1, part_count, send, 0)
            pltpu.make_async_remote_copy(
                src_ref=going.at[m, l], dst_ref=coming.at[m, l],
                send_sem=going_sem.at[m, l], recv_sem=coming_sem.at[m, l],
                device_id=(my_section, lax.rem(me + 1, part_count)), device_id_type=MESH,
            ).wait()

            def arrive(k, carry, l=l, now=now):
                table[now, 2 * tiles + k] = coming[m, l, k]
                return carry

            lax.fori_loop(0, others, arrive, 0)

            def quad(g, carry, l=l, now=now, later=later):
                parts = []
                for c in range(4):
                    at = (4 * g + c) * 4
                    pair = [
                        jnp.where(
                            low,
                            table[now, source_ref[l, at + 2 * h]],
                            table[now, source_ref[l, at + 2 * h + 1]],
                        )
                        for h in range(2)
                    ]
                    parts.append(jnp.concatenate(pair, axis=1))
                left = jnp.concatenate(parts, axis=0)
                summed = lax.dot_general(
                    left, held[l, g], (((1,), (1,)), ((), ())), preferred_element_type=jnp.float32
                )
                for t in range(2):
                    top = 2 * t * rows
                    cols = slice(t * lanes, (t + 1) * lanes)
                    pre_act = jnp.where(
                        low, summed[top : top + rows, cols], summed[top + rows : top + 2 * rows, cols]
                    )
                    pre_act = pre_act + bias_ref[l, 2 * g + t]
                    result = jnp.clip(pre_act, 0.0, 32.0)
                    if l == layer_count - 1:
                        outbox[m, 2 * g + t] = result.astype(jnp.bfloat16)
                    else:
                        table[later, 2 * (2 * g + t)] = result.astype(jnp.bfloat16)
                        table[later, 2 * (2 * g + t) + 1] = pltpu.roll(result, lanes // 2, 1).astype(jnp.bfloat16)
                return carry

            if l < layer_count - 1:
                lax.fori_loop(0, quads, quad, 0, unroll=4)
            else:
                for c in range(CHUNKS):
                    share = quads // CHUNKS
                    lax.fori_loop(c * share, (c + 1) * share, quad, 0, unroll=min(4, share))

                    @pl.when(my_section != last)
                    def _(c=c):
                        forward(m, c).start()

                    @pl.when((my_section == last) & (m != last))
                    def _(c=c):
                        deliver(m, c).start()

        return carry

    lax.fori_loop(0, micro_count, stage, 0)

    @pl.when(my_section == last)
    def _():
        own = pltpu.make_async_copy(outbox.at[last], out_ref, own_sem)
        own.start()
        own.wait()

    @pl.when(my_section != last)
    def _():
        for c in range(CHUNKS):
            deliver(0, c).wait_recv()

    @pl.when(my_section != 0)
    def _():
        for c in range(CHUNKS):
            feed(c).wait_send()

    def drain(m, carry):
        @pl.when((my_section != last) | (m != last))
        def _():
            for c in range(CHUNKS):
                forward(m, c).wait_send()

        return carry

    lax.fori_loop(0, micro_count, drain, 0)


def shards(images, weights, bias, pattern, counts):
    section_count = lax.axis_size("section")
    part_count = lax.axis_size("dom")
    my_part = lax.axis_index("dom")
    _, rows, width = images.shape
    layer_count, per_part, block_size, depth = weights.shape
    lanes = 2 * block_size
    tiles = width // lanes
    quads = per_part // 4
    others = part_count - 1
    micro_count = section_count * images.shape[0]
    wanted, source = prepare_tables(pattern, counts, per_part, part_count, my_part)
    tiled_images = images.reshape(rows, tiles, lanes).transpose(1, 0, 2)
    tiled_weights = weights.reshape(layer_count, quads, 4 * block_size, depth)
    tiled_bias = bias.astype(jnp.float32).reshape(layer_count, tiles, 1, lanes)
    in_vmem = pl.BlockSpec(memory_space=pltpu.VMEM)
    in_smem = pl.BlockSpec(memory_space=pltpu.SMEM)
    dma = pltpu.SemaphoreType.DMA
    flops = 2 * micro_count * layer_count * rows * per_part * block_size * depth
    result = pl.pallas_call(
        functools.partial(kernel, section_count, part_count),
        out_shape=jax.ShapeDtypeStruct((tiles, rows, lanes), jnp.bfloat16),
        in_specs=[in_smem, in_smem, in_vmem, pl.BlockSpec(memory_space=pl.ANY), in_vmem],
        out_specs=in_vmem,
        scratch_shapes=[
            pltpu.VMEM(tiled_weights.shape, jnp.bfloat16),
            pltpu.VMEM((micro_count, tiles, rows, lanes), jnp.bfloat16),
            pltpu.VMEM((micro_count, tiles, rows, lanes), jnp.bfloat16),
            pltpu.VMEM((2, 2 * tiles + part_count, rows, lanes), jnp.bfloat16),
            pltpu.VMEM((micro_count, layer_count, others, rows, lanes), jnp.bfloat16),
            pltpu.VMEM((micro_count, layer_count, others, rows, lanes), jnp.bfloat16),
            dma((layer_count,)),
            dma,
            dma((CHUNKS,)),
            dma((micro_count, CHUNKS)),
            dma((micro_count, CHUNKS)),
            dma((CHUNKS,)),
            dma((micro_count, layer_count)),
            dma((micro_count, layer_count)),
        ],
        compiler_params=pltpu.CompilerParams(
            collective_id=0, has_side_effects=True, vmem_limit_bytes=40 * 2**20
        ),
        cost_estimate=pl.CostEstimate(flops=flops, bytes_accessed=2 * weights.size, transcendentals=0),
    )(wanted, source, tiled_images, tiled_weights, tiled_bias)
    return result.transpose(1, 0, 2).reshape(1, rows, width)


def solution(mesh):
    placed = (
        P("section", None, "dom"),
        P("section", "dom", None, None),
        P("section", "dom"),
        P("section", None, None),
        P("section", "dom"),
    )
    return jax.shard_map(
        shards, mesh=mesh, in_specs=placed, out_specs=P("section", None, "dom"), check_vma=False
    )
```

time: 726 us -> 190 us (0.26)
  waiting for transfers between devices: 255 us -> 0 us
  local copies, waits for them, and re-layouts: 239 us -> 7.19 us
  Pallas kernels: 0 us -> 181 us
  other arithmetic: 85.3 us -> 1.73 us
  starting transfers between devices: 71.7 us -> 0 us
  matrix products: 52.6 us -> 0 us
  between operations: 13.5 us -> 0.06 us
    pallas_call x0 -> x1, Pallas kernels: none -> 181 us  [shards(): pl.pallas_call(functools.partial(kernel, section_count, part_count), out_...]
    reshape x42 -> x4, local copies, waits for them, and re-layouts: 106 us -> 2.31 us  [the longest x1 1.02 us: shards(): return result.transpose(1, 0, 2).reshape(1, rows, width)]
    psum x1 -> x0, waiting for transfers between devices: 85.3 us -> none  [spread(): return lax.psum(jnp.where(mine, x, jnp.zeros_like(x)), axis)]
    ppermute x7 -> x0, waiting for transfers between devices: 78.7 us -> none  [passed_along(): return lax.ppermute(x, axis, pairs)]
    all_to_all x14 -> x0, starting transfers between devices: 61.7 us -> none  [apply_layer(): lax.all_to_all(outgoing, 'dom', split_axis=1, concat_axis=1, tiled=True)]
    gather x28 -> x0, local copies, waits for them, and re-layouts: 56.4 us -> none  [the longest x14 48.5 us: apply_layer(): picked = jnp.take(pooled, layer_source.reshape(-1), axis=1)]
    select_n x37 -> x1, other arithmetic: 56.4 us -> 0.77 us  [prepare_tables(): jnp.where(slots < counts[:, :, None], source, per_part + part_count - 1)]
    all_to_all x14 -> x0, waiting for transfers between devices: 53.7 us -> none  [apply_layer(): lax.all_to_all(outgoing, 'dom', split_axis=1, concat_axis=1, tiled=True)]
  transfers between devices with their start and end apart: 23 -> 0, of which waited for: 23 -> 0; matrix products, arithmetic and copies ran while one was open for 4% -> 0% of each run, Pallas kernels for 0% -> 0%
where the time goes in v1:
time: 190 us
  Pallas kernels  181 us (95%)
  local copies, waits for them, and re-layouts  7.19 us (4%)
    pallas_call x1, Pallas kernels, shards(): pl.pallas_call(functools.partial(kernel, section_count, part_count), out_...  181 us
    unnamed x3, local copies, waits for them, and re-layouts  4.53 us

profile of v1, /device:TPU:25, one launch (start us, length us, event | category | flops | bytes accessed | tf_op | source)
XLA Modules:
  0.0 189.6 jit_solution(12794122004156578474)
XLA Ops:
  0.0 0.8 fusion.6
  0.8 0.9 fusion.2
  1.6 0.1 bitcast_reduce_fusion.wanted_ref
  1.7 0.8 reshape.32.bias_ref
  2.6 0.1 copy.10
  2.7 0.1 reshape.25.source_ref
  2.8 1.2 copy.14
  4.0 0.3 copy.17
  4.4 0.0 copy-start
  4.4 3.4 %copy-done = bf16[2,128,64,256]{3,2,1,0:T(8,128)(2,1)S(1)} copy-done((bf16[2,128,64,256]{3,2,1,0:T(8,128)(2,1)S(1)}, bf16[2,128,64,256]{3,2,1,0:T(8,128)(2,1)}, u32[]{:S(2)}) %copy-start) | copy-done | bytes 8388632
  7.7 180.6 %shard_map.55 = bf16[64,32,128]{2,1,0:T(8,128)(2,1)S(1)} custom-call(s32[2,8]{1,0:T(2,128)S(1)} %bitcast_reduce_fusion.wanted_ref, s32[2,512]{1,0:T(2,128)S(1)} %reshape.25.source_ref, bf16[64,32,128]{2,1,0:T(8,128)(2,1)S(1)} %bitcast.12, bf16[2,32,256,256]{3,2,1,0:T(8,128)(2,1)S(1)} %bitcast.11, f32[2,64,1,128]{3,2,1,0:T(1,128)S(1)} %reshape.32.bias_ref), custom_call_target="tpu_custom_call" | custom-call | flops 1073741824 | bytes 8388608 | tf_op jit(solution)/shard_map/pallas_call | solution.py:255
  188.3 0.2 copy.12
  188.5 1.0 reshape.30
  (1 shorter events, 0.0 us)
Async XLA Ops:
  4.4 3.4 %copy-start = (bf16[2,128,64,256]{3,2,1,0:T(8,128)(2,1)S(1)}, bf16[2,128,64,256]{3,2,1,0:T(8,128)(2,1)}, u32[]{:S(2)}) copy-start(bf16[2,128,64,256]{3,2,1,0:T(8,128)(2,1)} %param.6) | copy-start | bytes 25165828

commit v2 on v1

v2 whole, which is shorter than its diff:
```python
import functools

import jax
import jax.numpy as jnp
from jax import lax
from jax.experimental import pallas as pl
from jax.experimental.pallas import tpu as pltpu
from jax.sharding import PartitionSpec as P

MESH = pl.DeviceIdType.MESH
CHUNKS = 2
PIECE_ROWS = 16


def prepare_tables(pattern, counts, per_part, part_count, my_part):
    layer_count = pattern.shape[0]
    slot_count = pattern.shape[2]
    block_table = pattern.reshape(layer_count, part_count, per_part * slot_count)
    owners = block_table // per_part
    wanted = jnp.max(jnp.where(owners == my_part, block_table % per_part, 0), axis=2)
    own_rows = lax.dynamic_slice_in_dim(pattern, my_part * per_part, per_part, 1)
    own_owners = own_rows // per_part
    slots = jnp.arange(slot_count, dtype=jnp.int32)[None, None, :]
    local = (own_rows % per_part) ^ (slots & 1)
    remote = per_part + (my_part - own_owners + part_count) % part_count - 1
    source = jnp.where(own_owners == my_part, local, remote)
    source = jnp.where(slots < counts[:, :, None], source, per_part + part_count - 1)
    return wanted, source.reshape(layer_count, per_part * slot_count)


def kernel(
    section_count, part_count, halves, wanted_ref, source_ref, images_ref, weights_ref, bias_ref, out_ref,
    held, inbox, outbox, table, going, coming,
    weight_sem, own_sem, feed_sem, in_sem, out_sem, result_sem, going_sem, coming_sem, turn_sem,
):
    my_section = lax.axis_index("section")
    me = lax.axis_index("dom")
    layer_count, quads = weights_ref.shape[0], weights_ref.shape[1]
    piece_count, tiles, rows, lanes = inbox.shape
    per_chunk = tiles // CHUNKS
    share = quads // CHUNKS
    last = section_count - 1
    others = part_count - 1
    pieces = [(h, c) for h in range(halves) for c in range(CHUNKS)]

    loads = [
        pltpu.make_async_copy(weights_ref.at[l], held.at[l], weight_sem.at[l])
        for l in range(layer_count)
    ]
    for load in loads:
        load.start()

    barrier = pltpu.get_barrier_semaphore()

    def greet_part(step, carry):
        pl.semaphore_signal(
            barrier, inc=1, device_id=(my_section, lax.rem(me + step, part_count)), device_id_type=MESH
        )
        return carry

    def greet_section(step, carry):
        pl.semaphore_signal(
            barrier, inc=1, device_id=(lax.rem(my_section + step, section_count), me), device_id_type=MESH
        )
        return carry

    lax.fori_loop(1, part_count, greet_part, 0)
    lax.fori_loop(1, section_count, greet_section, 0)
    pl.semaphore_wait(barrier, others + section_count - 1)

    def chunk_of(c):
        return pl.ds(c * per_chunk, per_chunk)

    def feed(h, c):
        return pltpu.make_async_remote_copy(
            src_ref=images_ref.at[h, chunk_of(c)], dst_ref=inbox.at[my_section * halves + h, chunk_of(c)],
            send_sem=feed_sem.at[h, c], recv_sem=in_sem.at[my_section * halves + h, c],
            device_id=(0, me), device_id_type=MESH,
        )

    def forward(u, c):
        return pltpu.make_async_remote_copy(
            src_ref=outbox.at[u, chunk_of(c)], dst_ref=inbox.at[u, chunk_of(c)],
            send_sem=out_sem.at[u, c], recv_sem=in_sem.at[u, c],
            device_id=(lax.rem(my_section + 1, section_count), me), device_id_type=MESH,
        )

    def deliver(u, c):
        return pltpu.make_async_remote_copy(
            src_ref=outbox.at[u, chunk_of(c)], dst_ref=out_ref.at[lax.rem(u, halves), chunk_of(c)],
            send_sem=out_sem.at[u, c], recv_sem=result_sem.at[lax.rem(u, halves), c],
            device_id=(lax.div(u, halves), me), device_id_type=MESH,
        )

    @pl.when(my_section == 0)
    def _():
        own = pltpu.make_async_copy(images_ref, inbox.at[pl.ds(0, halves)], own_sem)
        own.start()
        own.wait()

    @pl.when(my_section > 1)
    def _():
        pl.semaphore_wait(turn_sem, 1)

    @pl.when(my_section != 0)
    def _():
        for h, c in pieces:
            feed(h, c).start()
        for h, c in pieces:
            feed(h, c).wait_send()

    @pl.when((my_section != 0) & (my_section != last))
    def _():
        pl.semaphore_signal(turn_sem, inc=1, device_id=(my_section + 1, me), device_id_type=MESH)

    low = lax.broadcasted_iota(jnp.int32, (rows, lanes), 1) < lanes // 2
    for l in range(layer_count):
        table[l, 2 * tiles + others] = jnp.zeros((rows, lanes), jnp.bfloat16)

    def turned(x):
        return pltpu.roll(x.astype(jnp.float32), lanes // 2, 1).astype(jnp.bfloat16)

    def exchange(u, l):
        return pltpu.make_async_remote_copy(
            src_ref=going.at[u, l], dst_ref=coming.at[u, l],
            send_sem=going_sem.at[u, l], recv_sem=coming_sem.at[u, l],
            device_id=(my_section, lax.rem(me + 1, part_count)), device_id_type=MESH,
        )

    def send(u, l):
        def one(step, carry):
            peer = lax.rem(me + step, part_count)
            block = wanted_ref[l, peer]
            going[u, l, step - 1] = jnp.where(low, table[l, block], table[l, block ^ 1])
            pltpu.make_async_remote_copy(
                src_ref=going.at[u, l, step - 1], dst_ref=coming.at[u, l, step - 1],
                send_sem=going_sem.at[u, l], recv_sem=coming_sem.at[u, l],
                device_id=(my_section, peer), device_id_type=MESH,
            ).start()
            return carry

        lax.fori_loop(1, part_count, one, 0)

    def enter(u):
        def tile(q, carry):
            x = inbox[u, q]
            table[0, 2 * q] = x
            table[0, 2 * q + 1] = turned(x)
            return carry

        @pl.when((my_section != 0) | (u >= halves))
        def _():
            for c in range(CHUNKS):
                forward(u, c).wait_recv()

        lax.fori_loop(0, tiles, tile, 0, unroll=8)
        send(u, 0)

    def layer(u, l):
        exchange(u, l).wait()

        def arrive(k, carry):
            table[l, 2 * tiles + k] = coming[u, l, k]
            return carry

        lax.fori_loop(0, others, arrive, 0)

        def quad(g, carry):
            parts = []
            for c in range(4):
                at = (4 * g + c) * 4
                pair = [
                    jnp.where(
                        low,
                        table[l, source_ref[l, at + 2 * h]],
                        table[l, source_ref[l, at + 2 * h + 1]],
                    )
                    for h in range(2)
                ]
                parts.append(jnp.concatenate(pair, axis=1))
            left = jnp.concatenate(parts, axis=0)
            summed = lax.dot_general(
                left, held[l, g], (((1,), (0,)), ((), ())), preferred_element_type=jnp.float32
            )
            for t in range(2):
                top = 2 * t * rows
                cols = slice(t * lanes, (t + 1) * lanes)
                pre_act = jnp.where(
                    low, summed[top : top + rows, cols], summed[top + rows : top + 2 * rows, cols]
                )
                pre_act = pre_act + bias_ref[l, 2 * g + t]
                result = jnp.clip(pre_act, 0.0, 32.0)
                if l == layer_count - 1:
                    outbox[u, 2 * g + t] = result.astype(jnp.bfloat16)
                else:
                    table[l + 1, 2 * (2 * g + t)] = result.astype(jnp.bfloat16)
                    table[l + 1, 2 * (2 * g + t) + 1] = pltpu.roll(result, lanes // 2, 1).astype(jnp.bfloat16)
            return carry

        if l < layer_count - 1:
            lax.fori_loop(0, quads, quad, 0, unroll=min(8, quads))
            send(u, l + 1)
        else:
            for c in range(CHUNKS):
                lax.fori_loop(c * share, (c + 1) * share, quad, 0, unroll=min(8, share))

                @pl.when(my_section != last)
                def _(c=c):
                    forward(u, c).start()

                @pl.when((my_section == last) & (u < last * halves))
                def _(c=c):
                    deliver(u, c).start()

    for l, load in enumerate(loads):
        load.wait()

        def flip(g, carry, l=l):
            held[l, g] = held[l, g].T
            return carry

        lax.fori_loop(0, quads, flip, 0)
    enter(0)

    def stage(u, carry):
        for l in range(layer_count):
            layer(u, l)
            if l == 0:

                @pl.when(u + 1 < piece_count)
                def _():
                    enter(u + 1)

        return carry

    lax.fori_loop(0, piece_count, stage, 0)

    @pl.when(my_section == last)
    def _():
        own = pltpu.make_async_copy(outbox.at[pl.ds(last * halves, halves)], out_ref, own_sem)
        own.start()
        own.wait()

    @pl.when(my_section != last)
    def _():
        for h, c in pieces:
            deliver(h, c).wait_recv()

    def drain(u, carry):
        @pl.when((my_section != last) | (u < last * halves))
        def _():
            for c in range(CHUNKS):
                forward(u, c).wait_send()

        return carry

    lax.fori_loop(0, piece_count, drain, 0)


def shards(images, weights, bias, pattern, counts):
    section_count = lax.axis_size("section")
    part_count = lax.axis_size("dom")
    my_part = lax.axis_index("dom")
    _, rows, width = images.shape
    layer_count, per_part, block_size, depth = weights.shape
    lanes = 2 * block_size
    halves = rows // PIECE_ROWS
    tiles = width // lanes
    quads = per_part // 4
    others = part_count - 1
    piece_count = section_count * halves
    wanted, source = prepare_tables(pattern, counts, per_part, part_count, my_part)
    tiled_images = images.reshape(halves, PIECE_ROWS, tiles, lanes).transpose(0, 2, 1, 3)
    tiled_weights = weights.reshape(layer_count, quads, 4 * block_size, depth)
    tiled_bias = bias.astype(jnp.float32).reshape(layer_count, tiles, 1, lanes)
    in_vmem = pl.BlockSpec(memory_space=pltpu.VMEM)
    in_smem = pl.BlockSpec(memory_space=pltpu.SMEM)
    dma = pltpu.SemaphoreType.DMA
    flops = 2 * section_count * layer_count * rows * per_part * block_size * depth
    result = pl.pallas_call(
        functools.partial(kernel, section_count, part_count, halves),
        out_shape=jax.ShapeDtypeStruct((halves, tiles, PIECE_ROWS, lanes), jnp.bfloat16),
        in_specs=[in_smem, in_smem, in_vmem, pl.BlockSpec(memory_space=pl.ANY), in_vmem],
        out_specs=in_vmem,
        scratch_shapes=[
            pltpu.VMEM(tiled_weights.shape, jnp.bfloat16),
            pltpu.VMEM((piece_count, tiles, PIECE_ROWS, lanes), jnp.bfloat16),
            pltpu.VMEM((piece_count, tiles, PIECE_ROWS, lanes), jnp.bfloat16),
            pltpu.VMEM((layer_count, 2 * tiles + part_count, PIECE_ROWS, lanes), jnp.bfloat16),
            pltpu.VMEM((piece_count, layer_count, others, PIECE_ROWS, lanes), jnp.bfloat16),
            pltpu.VMEM((piece_count, layer_count, others, PIECE_ROWS, lanes), jnp.bfloat16),
            dma((layer_count,)),
            dma,
            dma((halves, CHUNKS)),
            dma((piece_count, CHUNKS)),
            dma((piece_count, CHUNKS)),
            dma((halves, CHUNKS)),
            dma((piece_count, layer_count)),
            dma((piece_count, layer_count)),
            pltpu.SemaphoreType.REGULAR,
        ],
        compiler_params=pltpu.CompilerParams(
            collective_id=0, has_side_effects=True, vmem_limit_bytes=40 * 2**20
        ),
        cost_estimate=pl.CostEstimate(flops=flops, bytes_accessed=2 * weights.size, transcendentals=0),
    )(wanted, source, tiled_images, tiled_weights, tiled_bias)
    return result.transpose(0, 2, 1, 3).reshape(1, rows, width)


def solution(mesh):
    placed = (
        P("section", None, "dom"),
        P("section", "dom", None, None),
        P("section", "dom"),
        P("section", None, None),
        P("section", "dom"),
    )
    return jax.shard_map(
        shards, mesh=mesh, in_specs=placed, out_specs=P("section", None, "dom"), check_vma=False
    )
```

time: 190 us -> 183 us (0.963)
  Pallas kernels: 181 us -> 174 us
    pallas_call x1, Pallas kernels: 181 us -> 174 us  [shards(): pl.pallas_call(functools.partial(kernel, section_count, part_count, halve...]
where the time goes in v2:
time: 183 us
  Pallas kernels  174 us (95%)
  local copies, waits for them, and re-layouts  7.12 us (4%)
    pallas_call x1, Pallas kernels, shards(): pl.pallas_call(functools.partial(kernel, section_count, part_count, halve...  174 us
    unnamed x3, local copies, waits for them, and re-layouts  4.53 us

profile of v2, /device:TPU:25, one launch (start us, length us, event | category | flops | bytes accessed | tf_op | source)
XLA Modules:
  0.0 183.1 jit_solution(14858582344884450577)
XLA Ops:
  0.0 0.8 fusion.6
  0.8 0.9 fusion.2
  1.6 0.1 bitcast_reduce_fusion.wanted_ref
  1.7 0.8 reshape.32.bias_ref
  2.6 0.1 copy.10
  2.7 0.1 reshape.25.source_ref
  2.8 1.2 copy.14
  4.0 0.3 copy.17
  4.3 0.0 copy-start
  4.4 3.4 %copy-done = bf16[2,128,64,256]{3,2,1,0:T(8,128)(2,1)S(1)} copy-done((bf16[2,128,64,256]{3,2,1,0:T(8,128)(2,1)S(1)}, bf16[2,128,64,256]{3,2,1,0:T(8,128)(2,1)}, u32[]{:S(2)}) %copy-start) | copy-done | bytes 8388632
  7.7 174.2 %shard_map.55 = bf16[2,64,16,128]{3,2,1,0:T(8,128)(2,1)S(1)} custom-call(s32[2,8]{1,0:T(2,128)S(1)} %bitcast_reduce_fusion.wanted_ref, s32[2,512]{1,0:T(2,128)S(1)} %reshape.25.source_ref, bf16[2,64,16,128]{3,2,1,0:T(8,128)(2,1)S(1)} %bitcast.15, bf16[2,32,256,256]{3,2,1,0:T(8,128)(2,1)S(1)} %bitcast.14, f32[2,64,1,128]{3,2,1,0:T(1,128)S(1)} %reshape.32.bias_ref), custom_call_target="tpu_custom_call" | custom-call | flops 1073741824 | bytes 8388608 | tf_op jit(solution)/shard_map/pallas_call | solution.py:280
  181.9 0.1 copy.12
  182.1 1.0 reshape.30
  (1 shorter events, 0.0 us)
Async XLA Ops:
  4.3 3.4 %copy-start = (bf16[2,128,64,256]{3,2,1,0:T(8,128)(2,1)S(1)}, bf16[2,128,64,256]{3,2,1,0:T(8,128)(2,1)}, u32[]{:S(2)}) copy-start(bf16[2,128,64,256]{3,2,1,0:T(8,128)(2,1)} %param.6) | copy-start | bytes 25165828

commit v3 on v2

--- a/solution.py
+++ b/solution.py
@@ -30,8 +30,8 @@
 
 def kernel(
     section_count, part_count, halves, wanted_ref, source_ref, images_ref, weights_ref, bias_ref, out_ref,
-    held, inbox, outbox, table, going, coming,
-    weight_sem, own_sem, feed_sem, in_sem, out_sem, result_sem, going_sem, coming_sem, turn_sem,
+    held, inbox, outbox, going, coming,
+    weight_sem, own_sem, feed_sem, in_sem, out_sem, result_sem, going_sem, coming_sem, turn_sem, *tables,
 ):
     my_section = lax.axis_index("section")
     me = lax.axis_index("dom")
@@ -115,7 +115,7 @@
 
     low = lax.broadcasted_iota(jnp.int32, (rows, lanes), 1) < lanes // 2
     for l in range(layer_count):
-        table[l, 2 * tiles + others] = jnp.zeros((rows, lanes), jnp.bfloat16)
+        tables[l][2 * tiles + others] = jnp.zeros((rows, lanes), jnp.bfloat16)
 
     def turned(x):
         return pltpu.roll(x.astype(jnp.float32), lanes // 2, 1).astype(jnp.bfloat16)
@@ -131,7 +131,7 @@
         def one(step, carry):
             peer = lax.rem(me + step, part_count)
             block = wanted_ref[l, peer]
-            going[u, l, step - 1] = jnp.where(low, table[l, block], table[l, block ^ 1])
+            going[u, l, step - 1] = jnp.where(low, tables[l][block], tables[l][block ^ 1])
             pltpu.make_async_remote_copy(
                 src_ref=going.at[u, l, step - 1], dst_ref=coming.at[u, l, step - 1],
                 send_sem=going_sem.at[u, l], recv_sem=coming_sem.at[u, l],
@@ -139,13 +139,13 @@
             ).start()
             return carry
 
-        lax.fori_loop(1, part_count, one, 0)
+        lax.fori_loop(1, part_count, one, 0, unroll=min(7, others))
 
     def enter(u):
         def tile(q, carry):
             x = inbox[u, q]
-            table[0, 2 * q] = x
-            table[0, 2 * q + 1] = turned(x)
+            tables[0][2 * q] = x
+            tables[0][2 * q + 1] = turned(x)
             return carry
 
         @pl.when((my_section != 0) | (u >= halves))
@@ -160,10 +160,10 @@
         exchange(u, l).wait()
 
         def arrive(k, carry):
-            table[l, 2 * tiles + k] = coming[u, l, k]
+            tables[l][2 * tiles + k] = coming[u, l, k]
             return carry
 
-        lax.fori_loop(0, others, arrive, 0)
+        lax.fori_loop(0, others, arrive, 0, unroll=min(7, others))
 
         def quad(g, carry):
             parts = []
@@ -172,15 +172,15 @@
                 pair = [
                     jnp.where(
                         low,
-                        table[l, source_ref[l, at + 2 * h]],
-                        table[l, source_ref[l, at + 2 * h + 1]],
+                        tables[l][source_ref[l, at + 2 * h]],
+                        tables[l][source_ref[l, at + 2 * h + 1]],
                     )
                     for h in range(2)
                 ]
                 parts.append(jnp.concatenate(pair, axis=1))
             left = jnp.concatenate(parts, axis=0)
             summed = lax.dot_general(
-                left, held[l, g], (((1,), (0,)), ((), ())), preferred_element_type=jnp.float32
+                left, held[l, g], (((1,), (1,)), ((), ())), preferred_element_type=jnp.float32
             )
             for t in range(2):
                 top = 2 * t * rows
@@ -193,8 +193,8 @@
                 if l == layer_count - 1:
                     outbox[u, 2 * g + t] = result.astype(jnp.bfloat16)
                 else:
-                    table[l + 1, 2 * (2 * g + t)] = result.astype(jnp.bfloat16)
-                    table[l + 1, 2 * (2 * g + t) + 1] = pltpu.roll(result, lanes // 2, 1).astype(jnp.bfloat16)
+                    tables[l + 1][2 * (2 * g + t)] = result.astype(jnp.bfloat16)
+                    tables[l + 1][2 * (2 * g + t) + 1] = pltpu.roll(result, lanes // 2, 1).astype(jnp.bfloat16)
             return carry
 
         if l < layer_count - 1:
@@ -212,15 +212,9 @@
                 def _(c=c):
                     deliver(u, c).start()
 
-    for l, load in enumerate(loads):
+    enter(0)
+    for load in loads:
         load.wait()
-
-        def flip(g, carry, l=l):
-            held[l, g] = held[l, g].T
-            return carry
-
-        lax.fori_loop(0, quads, flip, 0)
-    enter(0)
 
     def stage(u, carry):
         for l in range(layer_count):
@@ -286,7 +280,6 @@
             pltpu.VMEM(tiled_weights.shape, jnp.bfloat16),
             pltpu.VMEM((piece_count, tiles, PIECE_ROWS, lanes), jnp.bfloat16),
             pltpu.VMEM((piece_count, tiles, PIECE_ROWS, lanes), jnp.bfloat16),
-            pltpu.VMEM((layer_count, 2 * tiles + part_count, PIECE_ROWS, lanes), jnp.bfloat16),
             pltpu.VMEM((piece_count, layer_count, others, PIECE_ROWS, lanes), jnp.bfloat16),
             pltpu.VMEM((piece_count, layer_count, others, PIECE_ROWS, lanes), jnp.bfloat16),
             dma((layer_count,)),
@@ -298,9 +291,10 @@
             dma((piece_count, layer_count)),
             dma((piece_count, layer_count)),
             pltpu.SemaphoreType.REGULAR,
-        ],
+        ]
+        + [pltpu.VMEM((2 * tiles + part_count, PIECE_ROWS, lanes), jnp.bfloat16)] * layer_count,
         compiler_params=pltpu.CompilerParams(
-            collective_id=0, has_side_effects=True, vmem_limit_bytes=40 * 2**20
+            collective_id=0, has_side_effects=True, vmem_limit_bytes=58 * 2**20
         ),
         cost_estimate=pl.CostEstimate(flops=flops, bytes_accessed=2 * weights.size, transcendentals=0),
     )(wanted, source, tiled_images, tiled_weights, tiled_bias)

time: 183 us -> 128 us (0.70)
  Pallas kernels: 174 us -> 119 us
    pallas_call x1, Pallas kernels: 174 us -> 119 us  [shards(): pl.pallas_call(functools.partial(kernel, section_count, part_count, halve...]
    unnamed x3 -> x1, local copies, waits for them, and re-layouts: 4.53 us -> 1.15 us
where the time goes in v3:
time: 128 us
  Pallas kernels  119 us (93%)
  local copies, waits for them, and re-layouts  6.79 us (5%)
  other arithmetic  2.31 us (2%)
    pallas_call x1, Pallas kernels, shards(): pl.pallas_call(functools.partial(kernel, section_count, part_count, halve...  119 us

profile of v3, /device:TPU:25, one launch (start us, length us, event | category | flops | bytes accessed | tf_op | source)
XLA Modules:
  0.0 127.9 jit_solution(12658750555227037919)
XLA Ops:
  0.0 0.8 fusion.6
  0.8 0.9 fusion.2
  1.6 0.7 bitcast_reduce_fusion.wanted_ref
  2.3 1.4 %reshape.32.bias_ref = f32[2,64,1,128]{3,2,1,0:T(1,128)} reshape(bf16[2,8192]{1,0:T(2,128)(2,1)} %param.7) | data formatting | bytes 98304 | tf_op jit(solution)/shard_map/reshape | solution.py:269
  3.8 0.1 copy.10
  3.9 0.7 reshape.25.source_ref
  4.6 1.2 copy.14
  5.8 1.1 copy.17
  6.9 118.8 %shard_map.55 = bf16[2,64,16,128]{3,2,1,0:T(8,128)(2,1)} custom-call(s32[2,8]{1,0:T(2,128)} %bitcast_reduce_fusion.wanted_ref, s32[2,512]{1,0:T(2,128)} %reshape.25.source_ref, bf16[2,64,16,128]{3,2,1,0:T(8,128)(2,1)} %bitcast.15, bf16[2,32,256,256]{3,2,1,0:T(8,128)(2,1)} %bitcast.14, f32[2,64,1,128]{3,2,1,0:T(1,128)} %reshape.32.bias_ref), custom_call_target="tpu_custom_call" | custom-call | flops 1073741824 | bytes 8388608 | tf_op jit(solution)/shard_map/pallas_call | solution.py:274
  125.7 1.2 copy.12
  126.9 1.0 reshape.30
  (1 shorter events, 0.0 us)

commit v4 on v3

--- a/solution.py
+++ b/solution.py
@@ -8,7 +8,7 @@
 from jax.sharding import PartitionSpec as P
 
 MESH = pl.DeviceIdType.MESH
-CHUNKS = 2
+CHUNKS = 4
 PIECE_ROWS = 16
 
 
@@ -30,7 +30,7 @@
 
 def kernel(
     section_count, part_count, halves, wanted_ref, source_ref, images_ref, weights_ref, bias_ref, out_ref,
-    held, inbox, outbox, going, coming,
+    held, flipped, inbox, outbox, going, coming,
     weight_sem, own_sem, feed_sem, in_sem, out_sem, result_sem, going_sem, coming_sem, turn_sem, *tables,
 ):
     my_section = lax.axis_index("section")
@@ -180,7 +180,7 @@
                 parts.append(jnp.concatenate(pair, axis=1))
             left = jnp.concatenate(parts, axis=0)
             summed = lax.dot_general(
-                left, held[l, g], (((1,), (1,)), ((), ())), preferred_element_type=jnp.float32
+                left, flipped[l, g], (((1,), (0,)), ((), ())), preferred_element_type=jnp.float32
             )
             for t in range(2):
                 top = 2 * t * rows
@@ -212,9 +212,15 @@
                 def _(c=c):
                     deliver(u, c).start()
 
+    for l, load in enumerate(loads):
+        load.wait()
+
+        def flip(g, carry, l=l):
+            flipped[l, g] = held[l, g].T
+            return carry
+
+        lax.fori_loop(0, quads, flip, 0, unroll=min(4, quads))
     enter(0)
-    for load in loads:
-        load.wait()
 
     def stage(u, carry):
         for l in range(layer_count):
@@ -278,6 +284,7 @@
         out_specs=in_vmem,
         scratch_shapes=[
             pltpu.VMEM(tiled_weights.shape, jnp.bfloat16),
+            pltpu.VMEM((layer_count, quads, depth, 4 * block_size), jnp.bfloat16),
             pltpu.VMEM((piece_count, tiles, PIECE_ROWS, lanes), jnp.bfloat16),
             pltpu.VMEM((piece_count, tiles, PIECE_ROWS, lanes), jnp.bfloat16),
             pltpu.VMEM((piece_count, layer_count, others, PIECE_ROWS, lanes), jnp.bfloat16),

time: 128 us -> 123 us (0.961)
  Pallas kernels: 119 us -> 113 us
    pallas_call x1, Pallas kernels: 119 us -> 113 us  [shards(): pl.pallas_call(functools.partial(kernel, section_count, part_count, halve...]
where the time goes in v4:
time: 123 us; the launch traced here: 122 us
  Pallas kernels  113 us (92%)
  local copies, waits for them, and re-layouts  6.79 us (6%)
  other arithmetic  2.31 us (2%)
    pallas_call x1, Pallas kernels, shards(): pl.pallas_call(functools.partial(kernel, section_count, part_count, halve...  113 us

profile of v4, /device:TPU:25, one launch (start us, length us, event | category | flops | bytes accessed | tf_op | source)
XLA Modules:
  0.0 122.2 jit_solution(12911009292014165061)
XLA Ops:
  0.0 0.8 fusion.6
  0.8 0.9 fusion.2
  1.6 0.7 bitcast_reduce_fusion.wanted_ref
  2.3 1.4 %reshape.32.bias_ref = f32[2,64,1,128]{3,2,1,0:T(1,128)} reshape(bf16[2,8192]{1,0:T(2,128)(2,1)} %param.7) | data formatting | bytes 98304 | tf_op jit(solution)/shard_map/reshape | solution.py:275
  3.8 0.1 copy.10
  3.9 0.7 reshape.25.source_ref
  4.6 1.2 copy.14
  5.8 1.1 copy.17
  6.9 113.1 %shard_map.55 = bf16[2,64,16,128]{3,2,1,0:T(8,128)(2,1)} custom-call(s32[2,8]{1,0:T(2,128)} %bitcast_reduce_fusion.wanted_ref, s32[2,512]{1,0:T(2,128)} %reshape.25.source_ref, bf16[2,64,16,128]{3,2,1,0:T(8,128)(2,1)} %bitcast.15, bf16[2,32,256,256]{3,2,1,0:T(8,128)(2,1)} %bitcast.14, f32[2,64,1,128]{3,2,1,0:T(1,128)} %reshape.32.bias_ref), custom_call_target="tpu_custom_call" | custom-call | flops 1073741824 | bytes 8388608 | tf_op jit(solution)/shard_map/pallas_call | solution.py:280
  120.0 1.2 copy.12
  121.2 1.0 reshape.30
  (1 shorter events, 0.0 us)

commit v5 on v4

--- a/solution.py
+++ b/solution.py
@@ -212,6 +212,10 @@
                 def _(c=c):
                     deliver(u, c).start()
 
+    @pl.when(my_section == 0)
+    def _():
+        enter(0)
+
     for l, load in enumerate(loads):
         load.wait()
 
@@ -220,7 +224,10 @@
             return carry
 
         lax.fori_loop(0, quads, flip, 0, unroll=min(4, quads))
-    enter(0)
+
+    @pl.when(my_section != 0)
+    def _():
+        enter(0)
 
     def stage(u, carry):
         for l in range(layer_count):

time: 123 us -> 119 us (0.967)
  Pallas kernels: 113 us -> 110 us
    pallas_call x1, Pallas kernels: 113 us -> 110 us  [shards(): pl.pallas_call(functools.partial(kernel, section_count, part_count, halve...]
where the time goes in v5:
time: 119 us
  Pallas kernels  110 us (92%)
  local copies, waits for them, and re-layouts  6.79 us (6%)
  other arithmetic  2.31 us (2%)
    pallas_call x1, Pallas kernels, shards(): pl.pallas_call(functools.partial(kernel, section_count, part_count, halve...  110 us

profile of v5, /device:TPU:25, one launch (start us, length us, event | category | flops | bytes accessed | tf_op | source)
XLA Modules:
  0.0 119.1 jit_solution(6196254689520029649)
XLA Ops:
  0.0 0.8 fusion.6
  0.8 0.9 fusion.2
  1.6 0.7 bitcast_reduce_fusion.wanted_ref
  2.3 1.4 %reshape.32.bias_ref = f32[2,64,1,128]{3,2,1,0:T(1,128)} reshape(bf16[2,8192]{1,0:T(2,128)(2,1)} %param.7) | data formatting | bytes 98304 | tf_op jit(solution)/shard_map/reshape | solution.py:282
  3.8 0.1 copy.10
  3.9 0.7 reshape.25.source_ref
  4.6 1.2 copy.14
  5.8 1.1 copy.17
  6.9 109.9 %shard_map.55 = bf16[2,64,16,128]{3,2,1,0:T(8,128)(2,1)} custom-call(s32[2,8]{1,0:T(2,128)} %bitcast_reduce_fusion.wanted_ref, s32[2,512]{1,0:T(2,128)} %reshape.25.source_ref, bf16[2,64,16,128]{3,2,1,0:T(8,128)(2,1)} %bitcast.15, bf16[2,32,256,256]{3,2,1,0:T(8,128)(2,1)} %bitcast.14, f32[2,64,1,128]{3,2,1,0:T(1,128)} %reshape.32.bias_ref), custom_call_target="tpu_custom_call" | custom-call | flops 1073741824 | bytes 8388608 | tf_op jit(solution)/shard_map/pallas_call | solution.py:287
  116.9 1.2 copy.12
  118.0 1.0 reshape.30
  (1 shorter events, 0.0 us)
